TPU v7x, 128 devices: a whole 4x4x4 slice. The times are simulated.
128 devices in a mesh: row: 16 (over x, z), col: 8 (over y, core).
Axes of the slice: x: 4, y: 4, z: 4, core: 2. Of those that a mesh axis runs over, the one named last changes fastest.
Arguments:
- blocks: bfloat16 [16, 8, 96, 256, 256], P('row', 'col'), may hold values from -6 to 6
- sketch: bfloat16 [262144, 128], P('col'), may hold values from -6 to 6
- block_row: int32 [16, 8, 96], P('row', 'col'), may hold values from 0 to 127, as said below
- block_col: int32 [16, 8, 96], P('row', 'col'), may hold values from 0 to 127
- counts: int32 [16, 8], P('row', 'col'), may hold values from 12 to 96, as said below
Outputs:
- q_scaled: float32 [524288, 128], P(('row', 'col'))
- z_out: float32 [8, 32768, 128], P('col', 'row')
Inputs may be any that keep to these rules, and one draw needn't show every extreme that they name: `block_row`: block row of a slot among the 128 block rows of its device. `counts`: slots at or beyond a device's count are not part of the matrix.
All inputs are finite; a program needn't handle non-finite values.
Results may differ from a plain program's by a relative error of at most 0.0019.
Values may be sent and summed in bfloat16 or wider, within the bound.
No kernel may reach another device: no remote copies, remote signals or barrier semaphores. Data moves between devices by JAX's collectives and lax.ppermute only.
A program may use at most 192 MiB of HBM per device.

v0:
```python
import math

import jax
import jax.numpy as jnp
from jax import lax
from jax.sharding import PartitionSpec as P

B = 256
K = 128
BR = 128
BC = 128


slot_batch = 8


def accumulate(tile_stack, source_index, target_index, live_total, table, targets, flipped):
    tile_size = tile_stack.shape[1]
    table_width = table.shape[2]

    def advance(turn_index, running):
        slot_start = turn_index * slot_batch
        tile_set = lax.dynamic_slice_in_dim(tile_stack, slot_start, slot_batch, 0)
        source_set = lax.dynamic_slice_in_dim(source_index, slot_start, slot_batch, 0)
        target_set = lax.dynamic_slice_in_dim(target_index, slot_start, slot_batch, 0)
        chosen = jnp.take(table, source_set, axis=0)
        if flipped:
            product = jnp.einsum(
                "gij,gik->gjk", tile_set, chosen, preferred_element_type=jnp.float32
            )
        else:
            product = jnp.einsum(
                "gij,gjk->gik", tile_set, chosen, preferred_element_type=jnp.float32
            )
        live_mask = (slot_start + jnp.arange(slot_batch, dtype=jnp.int32) < live_total).astype(
            jnp.float32
        )
        product = product * live_mask[:, None, None]
        for member in range(slot_batch):
            target = target_set[member]
            current = lax.dynamic_slice_in_dim(running, target, 1, 0)
            running = lax.dynamic_update_slice_in_dim(
                running, current + product[member][None], target, 0
            )
        return running

    turn_count = (live_total + slot_batch - 1) // slot_batch
    initial = jnp.zeros((targets, tile_size, table_width), jnp.float32)
    return lax.fori_loop(0, turn_count, advance, initial)


def body(blocks, sketch, block_row, block_col, counts):
    highest = lax.Precision.HIGHEST
    tile_stack = blocks[0, 0]
    row_slots = block_row[0, 0]
    col_slots = block_col[0, 0]
    live_total = counts[0, 0]
    sketch_table = sketch.reshape(BC, B, K)
    partial_y = accumulate(
        tile_stack, col_slots, row_slots, live_total, sketch_table, BR, False
    ).reshape(BR * B, K)
    y_share = lax.psum_scatter(partial_y, "col", scatter_dimension=0, tiled=True)
    local_gram = jnp.dot(y_share.T, y_share, precision=highest, preferred_element_type=jnp.float32)
    gram_sum = lax.psum(local_gram, ("row", "col"))
    lower_factor = jnp.linalg.cholesky(gram_sum)
    q_share = lax.linalg.triangular_solve(
        lower_factor, y_share, left_side=False, lower=True, transpose_a=True
    )
    q_group = lax.all_gather(q_share.astype(jnp.bfloat16), "col", axis=0, tiled=True)
    q_table = q_group.reshape(BR, B, K)
    partial_z = accumulate(tile_stack, row_slots, col_slots, live_total, q_table, BC, True).reshape(
        BC * B, K
    )
    z_share = lax.psum_scatter(partial_z, "row", scatter_dimension=0, tiled=True)
    row_scale = math.sqrt(BR * B * lax.axis_size("row"))
    return (q_share * row_scale, z_share[None])


def solution(mesh):
    in_specs = (
        P("row", "col", None, None, None),
        P("col", None),
        P("row", "col", None),
        P("row", "col", None),
        P("row", "col"),
    )
    out_specs = (P(("row", "col"), None), P("col", "row", None))
    return jax.shard_map(body, mesh=mesh, in_specs=in_specs, out_specs=out_specs, check_vma=False)
```

profile of v0, /device:TPU:24, one launch (start us, length us, event | category | flops | bytes accessed | tf_op | source)
XLA Modules:
  0.0 1294.4 jit_solution(14853689489823625723)
XLA Ops:
  7.9 7.8 broadcast.80.clone
  15.7 277.5 %while.20 = (s32[]{:T(128)}, f32[128,256,128]{2,1,0:T(8,128)}, s32[]{:T(128)}, s32[96]{0:T(128)S(1)}, bf16[96,256,256]{2,1,0:T(8,128)(2,1)}, /*index=5*/s32[96]{...) while((s32[]{:T(128)}, f32[128,256,128]{2,1,0:T(8,128)}, ...), condition=%wide.region_1.3_spmd, body=%wide.region_0.2_spmd.sunk | while | flops 135005264 | bytes 6820671 | solution.py:49
  32.1 4.0 gather_fusion
  36.1 1.7 convolution_multiply_fusion.4
  66.8 4.0 gather_fusion
  101.4 4.0 gather_fusion
  136.1 4.0 gather_fusion
  170.8 4.0 gather_fusion
  205.5 4.0 gather_fusion
  240.2 4.0 gather_fusion
  274.9 4.0 gather_fusion
  293.3 228.5 %reduce-scatter.3.cloned.1.call-done = f32[4096,128]{1,0:T(8,128)} async-done(((f32[32768,128]{1,0:T(8,128)}), f32[4096,128]{1,0:T(8,128)}) %reduce-scatter.3.cloned.1.call-update) | async-done | bytes 2097168 | tf_op jit(solution)/shard_map/reduce_scatter | solution.py:62
  521.9 6.3 fusion.35
  528.4 136.2 %all-reduce.2.cloned.1.call-done = f32[128,128]{0,1:T(8,128)} async-done(((f32[128,128]{0,1:T(8,128)}), f32[128,128]{0,1:T(8,128)}) %all-reduce.2.cloned.1.call-update) | async-done | bytes 65552 | tf_op jit(solution)/shard_map/psum | solution.py:64
  666.4 11.7 cholesky.16
  679.5 9.8 custom-call.6
  689.3 5.0 fusion.34
  694.4 16.7 %copy.7 = bf16[1,1,96,256,256]{3,4,2,1,0:T(8,128)(2,1)} copy(bf16[1,1,96,256,256]{4,3,2,1,0:T(8,128)(2,1)} %bitcast.76) | data formatting | bytes 25165824 | tf_op args[0]
  711.1 31.1 %all-gather.2.cloned.1.call-done = bf16[32768,128]{1,0:T(8,128)(2,1)} async-done(((bf16[4096,128]{1,0:T(8,128)(2,1)}), bf16[32768,128]{1,0:T(8,128)(2,1)}) %all-gather.2.cloned.1.call-update) | async-done | bytes 8388624 | tf_op jit(solution)/shard_map/all_gather | solution.py:69
  742.2 7.8 broadcast.80
  750.0 284.5 %while.21 = (s32[]{:T(128)}, f32[128,256,128]{2,1,0:T(8,128)}, s32[]{:T(128)}, s32[96]{0:T(128)S(1)}, bf16[96,256,256]{1,2,0:T(8,128)(2,1)}, /*index=5*/s32[96]{...) while((s32[]{:T(128)}, f32[128,256,128]{2,1,0:T(8,128)}, ...), condition=%wide.region_7.9_spmd, body=%wide.region_6.8_spmd.sunk | while | flops 135005264 | bytes 6820671 | solution.py:49
  767.2 4.0 gather_fusion.1
  771.3 1.7 convolution_multiply_fusion.5
  802.8 4.0 gather_fusion.1
  838.3 4.0 gather_fusion.1
  873.9 4.0 gather_fusion.1
  909.5 4.0 gather_fusion.1
  945.0 4.0 gather_fusion.1
  949.0 1.7 convolution_multiply_fusion.5
  980.6 4.0 gather_fusion.1
  1016.2 4.0 gather_fusion.1
  1034.6 253.3 %reduce-scatter.5.cloned.1.call-done = f32[2048,128]{1,0:T(8,128)} async-done(((f32[32768,128]{1,0:T(8,128)}), f32[2048,128]{1,0:T(8,128)}) %reduce-scatter.5.cloned.1.call-update) | async-done | bytes 1048592 | tf_op jit(solution)/shard_map/reduce_scatter | solution.py:74
  (222 shorter events, 251.1 us)
Async XLA Ops:
  7.2 8.6 copy-start.1
  7.2 8.6 copy-start
  7.2 514.7 %reduce-scatter.3.cloned.1.call-start = ((), (), s32[]{:S(2)}) async-start(), calls=%async_computation.2 | async-start | bytes 18874368 | tf_op jit(solution)/shard_map/reduce_scatter | solution.py:62
  293.3 371.3 %all-reduce.2.cloned.1.call-start = ((), (), s32[]{:S(2)}) async-start(), calls=%async_computation.3 | async-start | bytes 131072 | tf_op jit(solution)/shard_map/psum | solution.py:64
  528.2 214.0 %all-gather.2.cloned.1.call-start = ((), (), s32[]{:S(2)}) async-start(), calls=%async_computation.4 | async-start | bytes 9437184 | tf_op jit(solution)/shard_map/all_gather | solution.py:69
  694.3 593.6 %reduce-scatter.5.cloned.1.call-start = ((), (), s32[]{:S(2)}) async-start(), calls=%async_computation.5 | async-start | bytes 17825792 | tf_op jit(solution)/shard_map/reduce_scatter | solution.py:74
Sparse Core Ops, SparseCore 0:
  293.4 228.4 reduce-scatter.2
  528.3 136.2 all-reduce.1
  694.5 47.6 all-gather.1
  1034.7 253.1 reduce-scatter.4
where the time goes:
time: 1310 us; the launch traced here: 1290 us
  waiting for transfers between devices  649 us (50%)
  loops' own time  245 us (19%)
  other arithmetic  237 us (18%)
  local copies, waits for them, and re-layouts  110 us (8%)
  matrix products  38.9 us (3%)
  between operations  14.5 us (1%)
    reduce_scatter x1, waiting for transfers between devices, body(): lax.psum_scatter(partial_z, 'row', scatter_dimension=0, tiled=True)  253 us
    another operation x2, loops' own time, accumulate(): return lax.fori_loop(0, turn_count, advance, initial)  245 us
    reduce_scatter x1, waiting for transfers between devices, body(): lax.psum_scatter(partial_y, 'col', scatter_dimension=0, tiled=True)  229 us
    dynamic_update_slice x128, other arithmetic, advance(): lax.dynamic_update_slice_in_dim(running, current + product[member][None],...  201 us
    psum x1, waiting for transfers between devices, body(): gram_sum = lax.psum(local_gram, ('row', 'col'))  136 us
    gather x16, local copies, waits for them, and re-layouts, advance(): chosen = jnp.take(table, source_set, axis=0)  64.5 us
    all_gather x1, waiting for transfers between devices, body(): lax.all_gather(q_share.astype(jnp.bfloat16), 'col', axis=0, tiled=True)  31.1 us
  transfers between devices with their start and end apart: 4, of which 4 were waited for; matrix products, arithmetic and copies ran while one was open for 1% of the time, Pallas kernels for 0%

commit v1 on v0

v1 whole, which is shorter than its diff:
```python
import math

import jax
import jax.numpy as jnp
from jax import lax
from jax.experimental import pallas as pl
from jax.experimental.pallas import tpu as pltpu
from jax.sharding import PartitionSpec as P

B = 256
K = 128
BR = 128
BC = 128
NBLK = 96
AHEAD = 24
VMEM_BYTES = 56 * 1024 * 1024
f32 = jnp.float32
f16 = jnp.float16


def ring(shift):
    return [(c, ((c // 2 + shift) % 4) * 2 + c % 2) for c in range(8)]


def along_x(shift):
    return [(r, ((r // 4 + shift) % 4) * 4 + r % 4) for r in range(16)]


def along_z(shift):
    return [(r, (r // 4) * 4 + (r % 4 + shift) % 4) for r in range(16)]


PAIR = [(c, c ^ 1) for c in range(8)]


def y_kernel(rows, cols, info, blocks, sketch, out, stat, order, block_buf, sketch_buf, sems):
    count, core, here = info[0], info[1], info[2]

    def pick(s, n):
        order[n] = s
        return n + jnp.where(((rows[s] >> 4) & 1) == core, 1, 0)

    order[0] = 0
    total = lax.fori_loop(0, count, pick, 0)

    def copies(j):
        s = order[j]
        return (
            pltpu.make_async_copy(blocks.at[s], block_buf.at[j], sems.at[0, j]),
            pltpu.make_async_copy(sketch.at[cols[s]], sketch_buf.at[j], sems.at[1, j]),
        )

    def begin(j, _):
        for copy in copies(j):
            copy.start()
        return 0

    lax.fori_loop(0, jnp.minimum(total, AHEAD), begin, 0)

    def clear(t, _):
        out[t] = jnp.zeros((B, K), f32)
        return 0

    lax.fori_loop(0, BR // 2, clear, 0)

    def step(j, carry):
        bound, largest = carry

        @pl.when(j + AHEAD < total)
        def _():
            begin(j + AHEAD, 0)

        for copy in copies(j):
            copy.wait()
        row = rows[order[j]]
        target = ((((row >> 5) - here) & 3) << 4) | (row & 15)
        tile = block_buf[j]
        product = jnp.dot(tile, sketch_buf[j], preferred_element_type=f32)
        out[target] += product
        bound = bound + jnp.max(jnp.abs(product).reshape(B // 8, 8, K), axis=0)
        largest = jnp.maximum(largest, jnp.max(jnp.abs(tile).reshape(B // 16, 16, B), axis=0))
        return bound, largest

    bound, largest = lax.fori_loop(
        0, total, step, (jnp.zeros((8, K), f32), jnp.zeros((16, B), jnp.bfloat16))
    )
    stat[0] = bound
    wide = largest.astype(f32)
    stat[1] = jnp.maximum(
        jnp.maximum(wide[:8, :K], wide[8:, :K]), jnp.maximum(wide[:8, K:], wide[8:, K:])
    )


def partial_rows(rows, cols, info, blocks, sketch):
    return pl.pallas_call(
        y_kernel,
        out_shape=(
            jax.ShapeDtypeStruct((BR // 2, B, K), f32),
            jax.ShapeDtypeStruct((2, 8, K), f32),
        ),
        in_specs=[pl.BlockSpec(memory_space=pltpu.SMEM)] * 3
        + [pl.BlockSpec(memory_space=pl.ANY)] * 2,
        out_specs=(
            pl.BlockSpec(memory_space=pltpu.VMEM),
            pl.BlockSpec(memory_space=pltpu.VMEM),
        ),
        scratch_shapes=[
            pltpu.SMEM((NBLK + 1,), jnp.int32),
            pltpu.VMEM((NBLK, B, B), jnp.bfloat16),
            pltpu.VMEM((NBLK, B, K), jnp.bfloat16),
            pltpu.SemaphoreType.DMA((2, NBLK)),
        ],
        compiler_params=pltpu.CompilerParams(vmem_limit_bytes=VMEM_BYTES),
        cost_estimate=pl.CostEstimate(
            flops=NBLK * B * B * K, bytes_accessed=18 * 1024 * 1024, transcendentals=0
        ),
        name="partial_rows",
    )(rows, cols, info, blocks, sketch)


def z_kernel(half, rows, cols, info, blocks, *rest):
    tables, (out, order, block_buf, y_buf, sems) = rest[:16], rest[16:]
    count, core, here_y, here_x, here_z = info[0], info[1], info[2], info[3], info[4]

    def pick(s, n):
        order[n] = s
        return n + jnp.where(((cols[s] >> 2) & 1) == half, 1, 0)

    order[0] = 0
    total = lax.fori_loop(0, count, pick, 0)

    def block_copy(j):
        return pltpu.make_async_copy(blocks.at[order[j]], block_buf.at[j], sems.at[0, j])

    def y_copy(j, table, inner):
        return pltpu.make_async_copy(table.at[inner], y_buf.at[j], sems.at[1, j])

    def begin(j, _):
        block_copy(j).start()
        row = rows[order[j]]
        source = (
            ((((row >> 4) & 1) ^ core) << 3) | ((((row >> 5) - here_y) & 3) << 1) | ((row >> 3) & 1)
        )

        def choose(low, size):
            if size == 1:
                y_copy(j, tables[low], row & 7).start()
                return
            mid = low + size // 2
            pl.when(source < mid)(lambda: choose(low, size // 2))
            pl.when(source >= mid)(lambda: choose(mid, size // 2))

        choose(0, 16)
        return 0

    lax.fori_loop(0, jnp.minimum(total, AHEAD), begin, 0)

    def clear(t, _):
        out[t] = jnp.zeros((B, K), f32)
        return 0

    lax.fori_loop(0, BC // 2, clear, 0)

    def step(j, _):
        @pl.when(j + AHEAD < total)
        def _():
            begin(j + AHEAD, 0)

        block_copy(j).wait()
        y_copy(j, tables[0], 0).wait()
        col = cols[order[j]]
        rel_x = ((col >> 5) - here_x) & 3
        rel_z = ((col >> 3) - here_z) & 3
        if half == 0:
            target = (rel_x << 4) | (rel_z << 2) | (col & 3)
        else:
            target = (rel_z << 4) | (rel_x << 2) | (col & 3)
        value = y_buf[j]
        high = value.astype(jnp.bfloat16)
        low = (value - high.astype(f32)).astype(jnp.bfloat16)
        both = jnp.concatenate([high, low], axis=1)
        product = lax.dot_general(
            block_buf[j], both, (((0,), (0,)), ((), ())), preferred_element_type=f32
        )
        out[target] += product[:, :K] + product[:, K:]
        return 0

    lax.fori_loop(0, total, step, 0)


def partial_cols(half, rows, cols, info, blocks, tables):
    def kernel(*refs):
        z_kernel(half, *refs)

    return pl.pallas_call(
        kernel,
        out_shape=jax.ShapeDtypeStruct((BC // 2, B, K), f32),
        in_specs=[pl.BlockSpec(memory_space=pltpu.SMEM)] * 3
        + [pl.BlockSpec(memory_space=pl.ANY)] * 17,
        out_specs=pl.BlockSpec(memory_space=pltpu.VMEM),
        scratch_shapes=[
            pltpu.SMEM((NBLK + 1,), jnp.int32),
            pltpu.VMEM((NBLK, B, B), jnp.bfloat16),
            pltpu.VMEM((NBLK, B, K), f32),
            pltpu.SemaphoreType.DMA((2, NBLK)),
        ],
        compiler_params=pltpu.CompilerParams(vmem_limit_bytes=VMEM_BYTES),
        cost_estimate=pl.CostEstimate(
            flops=NBLK * B * B * K * 2, bytes_accessed=22 * 1024 * 1024, transcendentals=0
        ),
        name="partial_cols",
    )(rows, cols, info, blocks, *tables)


def scale_for(bound):
    return jnp.exp2(jnp.ceil(jnp.log2(jnp.maximum(bound, 1e-30))) - 15.0)


def ring_sum(pieces, send, scale):
    inverse = 1.0 / scale

    def pack(value):
        return (value * inverse).astype(f16)

    def unpack(value):
        return value.astype(f32) * scale

    far_up = send(pack(pieces[2][0]), 1)
    far_down = send(pack(pieces[2][1]), -1)
    near_up = send(pack(pieces[1][1]), 1)
    near_down = send(pack(pieces[3][0]), -1)
    sum_up = send(pack(pieces[1][0] + unpack(far_up)), 1)
    sum_down = send(pack(pieces[3][1] + unpack(far_down)), -1)
    return (
        pieces[0][0] + unpack(near_down) + unpack(sum_up),
        pieces[0][1] + unpack(near_up) + unpack(sum_down),
    )


def body(blocks, sketch, block_row, block_col, counts):
    highest = lax.Precision.HIGHEST
    blocks = blocks[0, 0]
    rows, cols = block_row[0, 0], block_col[0, 0]
    count = counts[0, 0]
    row_at, col_at = lax.axis_index("row"), lax.axis_index("col")
    here_x, here_z = row_at // 4, row_at % 4
    here_y, core = col_at // 2, col_at % 2
    sketch_table = sketch.reshape(BC, B, K)

    def send_core(value):
        return lax.ppermute(value, "col", PAIR)

    def send_y(value, shift):
        return lax.ppermute(value, "col", ring(shift))

    def send_x(value, shift):
        return lax.ppermute(value, "row", along_x(shift))

    def send_z(value, shift):
        return lax.ppermute(value, "row", along_z(shift))

    other_half, other_stat = partial_rows(
        rows, cols, jnp.stack([count, 1 - core, here_y]), blocks, sketch_table
    )
    from_pair = send_core(other_half)
    own_half, own_stat = partial_rows(
        rows, cols, jnp.stack([count, core, here_y]), blocks, sketch_table
    )
    stat = jnp.maximum(other_stat, own_stat)
    block_max = jnp.max(stat[1])
    bound = jnp.full((8, K), jnp.max(stat[0]))
    bound = jnp.maximum(bound, send_core(bound))
    bound = jnp.maximum(
        jnp.maximum(bound, send_y(bound, 2)), jnp.maximum(send_y(bound, 1), send_y(bound, -1))
    )
    y_scale = scale_for(bound[0, 0] * 8.0)

    own_part = own_half.reshape(4, 2, 8 * B, K)
    pair_part = from_pair.reshape(4, 2, 8 * B, K)
    pieces = [tuple(own_part[r, h] + pair_part[r, h] for h in range(2)) for r in range(4)]
    y_first, y_second = ring_sum(pieces, send_y, y_scale)

    mine = [((v / y_scale).astype(f16)) for v in (y_first, y_second)]
    below = [send_y(mine[0], 1), None]
    above = [None, send_y(mine[1], -1)]
    below[1] = send_y(mine[1], 1)
    above[0] = send_y(mine[0], -1)
    across = [send_y(below[0], 1), send_y(above[1], -1)]
    own_core = [mine, above, across, below]
    pair_core = [[send_core(v) for v in part] for part in own_core]
    tables = [
        (v.astype(f32) * y_scale).reshape(8, B, K)
        for side in (own_core, pair_core)
        for part in side
        for v in part
    ]

    y_share = jnp.concatenate([y_first, y_second], axis=0)
    gram = jnp.dot(y_share.T, y_share, precision=highest, preferred_element_type=f32)
    y_max = jnp.max(jnp.abs(y_share))
    limits = jnp.concatenate([jnp.full((8, K), y_max), jnp.full((8, K), block_max)], axis=0)
    for axis, perm in (
        ("col", PAIR),
        ("col", [(c, c ^ 2) for c in range(8)]),
        ("col", [(c, c ^ 4) for c in range(8)]),
        ("row", [(r, r ^ 1) for r in range(16)]),
        ("row", [(r, r ^ 2) for r in range(16)]),
        ("row", [(r, r ^ 4) for r in range(16)]),
        ("row", [(r, r ^ 8) for r in range(16)]),
    ):
        got = lax.ppermute(jnp.concatenate([gram, limits], axis=0), axis, perm)
        gram = gram + got[:K]
        limits = jnp.maximum(limits, got[K:])
    z_scale = scale_for(limits[0, 0] * limits[8, 0] * (16.0 * NBLK * B))

    info = jnp.stack([count, core, here_y, here_x, here_z])
    half_a = partial_cols(0, rows, cols, info, blocks, tables)
    half_b = partial_cols(1, rows, cols, info, blocks, tables)

    def two_stage(partial, send_one, send_two):
        parts = partial.reshape(4, 2, 2, 4 * B, K)
        firsts = ring_sum(
            [tuple(parts[r, h].reshape(2 * 4 * B, K) for h in range(2)) for r in range(4)],
            send_one,
            z_scale,
        )
        firsts = [v.reshape(2, 2, 2 * B, K) for v in firsts]
        return ring_sum(
            [tuple(firsts[r // 2][r % 2, h] for h in range(2)) for r in range(4)], send_two, z_scale
        )

    z_a = two_stage(half_a, send_x, send_z)
    z_b = two_stage(half_b, send_z, send_x)

    lower_factor = jnp.linalg.cholesky(gram)
    inverse = lax.linalg.triangular_solve(
        lower_factor, jnp.eye(K, dtype=f32), left_side=True, lower=True
    )
    q_share = jnp.dot(y_share, inverse.T, precision=highest, preferred_element_type=f32)
    z_raw = jnp.concatenate([*z_a, *z_b], axis=0)
    z_share = jnp.dot(z_raw, inverse.T, precision=highest, preferred_element_type=f32)
    row_scale = math.sqrt(BR * B * lax.axis_size("row"))
    return (q_share * row_scale, z_share[None])


def solution(mesh):
    in_specs = (
        P("row", "col", None, None, None),
        P("col", None),
        P("row", "col", None),
        P("row", "col", None),
        P("row", "col"),
    )
    out_specs = (P(("row", "col"), None), P("col", "row", None))
    return jax.shard_map(body, mesh=mesh, in_specs=in_specs, out_specs=out_specs, check_vma=False)
```

time: 1310 us -> 353 us (0.27)
  waiting for transfers between devices: 649 us -> 115 us
  loops' own time: 245 us -> 0 us
  other arithmetic: 237 us -> 74.2 us
  local copies, waits for them, and re-layouts: 110 us -> 5.55 us
  starting transfers between devices: 0.34 us -> 95.2 us
  Pallas kernels: 0 us -> 43.2 us
  matrix products: 38.9 us -> 8.8 us
    reduce_scatter x2 -> x0, waiting for transfers between devices: 482 us -> none  [the longest x1 253 us: body(): lax.psum_scatter(partial_z, 'row', scatter_dimension=0, tiled=True)]
    another operation x2 -> x0, loops' own time: 245 us -> none  [accumulate(): return lax.fori_loop(0, turn_count, advance, initial)]
    dynamic_update_slice x128 -> x0, other arithmetic: 201 us -> none  [advance(): lax.dynamic_update_slice_in_dim(running, current + product[member][None],...]
    psum x1 -> x0, waiting for transfers between devices: 136 us -> none  [body(): gram_sum = lax.psum(local_gram, ('row', 'col'))]
    ppermute x0 -> x56, waiting for transfers between devices: none -> 115 us  [the longest x15 50.4 us: send_y(): return lax.ppermute(value, 'col', ring(shift))]
    ppermute x0 -> x56, starting transfers between devices: none -> 95.2 us  [the longest x12 33.2 us: send_x(): return lax.ppermute(value, 'row', along_x(shift))]
    gather x16 -> x0, local copies, waits for them, and re-layouts: 64.5 us -> none  [advance(): chosen = jnp.take(table, source_set, axis=0)]
    pallas_call x0 -> x4, Pallas kernels: none -> 43.2 us  [the longest x2 26.5 us: partial_cols(): pl.pallas_call(kernel, out_shape=jax.ShapeDtypeStruct((BC // 2, B, K), f3...]
  transfers between devices with their start and end apart: 4 -> 56, of which waited for: 4 -> 26; matrix products, arithmetic and copies ran while one was open for 1% -> 19% of each run, Pallas kernels for 0% -> 5%
where the time goes in v1:
time: 353 us; the launch traced here: 348 us
  waiting for transfers between devices  115 us (33%)
  starting transfers between devices  95.2 us (27%)
  other arithmetic  74.2 us (21%)
  Pallas kernels  43.2 us (12%)
  matrix products  8.8 us (2%)
  between operations  6.27 us (2%)
  local copies, waits for them, and re-layouts  5.55 us (2%)
    ppermute x15, waiting for transfers between devices, send_y(): return lax.ppermute(value, 'col', ring(shift))  50.4 us
    ppermute x12, starting transfers between devices, send_x(): return lax.ppermute(value, 'row', along_x(shift))  33.2 us
    mul x16, other arithmetic, body(): v.astype(f32) * y_scale  26.8 us
    pallas_call x2, Pallas kernels, partial_cols(): pl.pallas_call(kernel, out_shape=jax.ShapeDtypeStruct((BC // 2, B, K), f3...  26.5 us
    ppermute x12, waiting for transfers between devices, send_x(): return lax.ppermute(value, 'row', along_x(shift))  26.5 us
    ppermute x7, starting transfers between devices, body(): got = lax.ppermute(jnp.concatenate([gram, limits], axis=0), axis, perm)  26.4 us
    ppermute x12, waiting for transfers between devices, send_z(): return lax.ppermute(value, 'row', along_z(shift))  17.9 us
    ppermute x7, waiting for transfers between devices, body(): got = lax.ppermute(jnp.concatenate([gram, limits], axis=0), axis, perm)  17.7 us
  transfers between devices with their start and end apart: 56, of which 26 were waited for; matrix products, arithmetic and copies ran while one was open for 19% of the time, Pallas kernels for 5%

profile of v1, /device:TPU:24, one launch (start us, length us, event | category | flops | bytes accessed | tf_op | source)
XLA Modules:
  0.0 347.8 jit_solution(7988652615028626581)
XLA Ops:
  2.0 8.1 %partial_rows.3 = (f32[64,256,128]{2,1,0:T(8,128)}, f32[2,8,128]{2,1,0:T(8,128)}) custom-call(s32[96]{0:T(128)} %bitcast.271, s32[96]{0:T(128)} %bitcast.275, s32[3]{0:T(128)} %get-tuple-element.52.info, bf16[96,256,256]{2,1,0:T(8,128)(2,1)} %bitcast.209, bf16[128,256,128]{2,1,0:T(8,128)(2,1)} %bitcast.213), custom_call_target="tpu_custom_call" | custom-call | flops 805306368 | bytes 18874368 | tf_op jit(solution)/shard_map/partial_rows/pallas_call | solution.py:95
  10.9 8.6 %partial_rows.2 = (f32[64,256,128]{2,1,0:T(8,128)}, f32[2,8,128]{2,1,0:T(8,128)}) custom-call(s32[96]{0:T(128)} %bitcast.272, s32[96]{0:T(128)} %bitcast.276, s32[3]{0:T(128)} %get-tuple-element.51.info, bf16[96,256,256]{2,1,0:T(8,128)(2,1)} %bitcast.210, bf16[128,256,128]{2,1,0:T(8,128)(2,1)} %bitcast.214), custom_call_target="tpu_custom_call" | custom-call | flops 805306368 | bytes 18874368 | tf_op jit(solution)/shard_map/partial_rows/pallas_call | solution.py:95
  35.0 4.1 %fusion.50 = (f16[2048,128]{1,0:T(8,128)(2,1)S(1)}, f16[2048,128]{1,0:T(8,128)(2,1)S(1)}, f16[2048,128]{1,0:T(8,128)(2,1)S(1)}, f16[2048,128]{1,0:T(8,128)(2,1)S(1)}) fusion(f32[4,2,2048,128]{3,2,1,0:T(8,128)} %bitcast.9, f32[4,2,2048,128]{3,2,1,0:T(8,128)} %bitcast.249, f32[]{:T(128)S(6)} %div.43), kind=kLoop, calls=%fused_computation.96 | loop fusion | flops 3145728 | bytes 10485764 | tf_op jit(solution)/shard_map/convert_element_type | solution.py:223
  41.5 11.0 %collective-permute-done.6 = f16[2048,128]{1,0:T(8,128)(2,1)S(1)} collective-permute-done((f16[2048,128]{1,0:T(8,128)(2,1)S(1)}, f16[2048,128]{1,0:T(8,128)(2,1)S(1)}, u32[]{:S(2)}, u32[]{:S(2)}) %collective-permute-start.6) | collective-permute-done | bytes 524320 | tf_op jit(solution)/shard_map/ppermute | solution.py:254
  56.1 9.1 %collective-permute-done.9 = f16[2048,128]{1,0:T(8,128)(2,1)S(1)} collective-permute-done((f16[2048,128]{1,0:T(8,128)(2,1)S(1)}, f16[2048,128]{1,0:T(8,128)(2,1)S(1)}, u32[]{:S(2)}, u32[]{:S(2)}) %collective-permute-start.9) | collective-permute-done | bytes 524320 | tf_op jit(solution)/shard_map/ppermute | solution.py:254
  65.2 3.8 %collective-permute-done.7 = f16[2048,128]{1,0:T(8,128)(2,1)S(1)} collective-permute-done((f16[2048,128]{1,0:T(8,128)(2,1)S(1)}, f16[2048,128]{1,0:T(8,128)(2,1)S(1)}, u32[]{:S(2)}, u32[]{:S(2)}) %collective-permute-start.7) | collective-permute-done | bytes 524320 | tf_op jit(solution)/shard_map/ppermute | solution.py:254
  72.9 4.9 %collective-permute-done.8 = f16[2048,128]{1,0:T(8,128)(2,1)S(1)} collective-permute-done((f16[2048,128]{1,0:T(8,128)(2,1)S(1)}, f16[2048,128]{1,0:T(8,128)(2,1)S(1)}, u32[]{:S(2)}, u32[]{:S(2)}) %collective-permute-start.8) | collective-permute-done | bytes 524320 | tf_op jit(solution)/shard_map/ppermute | solution.py:254
  77.8 4.7 %collective-permute-done.10 = f16[2048,128]{1,0:T(8,128)(2,1)S(1)} collective-permute-done((f16[2048,128]{1,0:T(8,128)(2,1)S(1)}, f16[2048,128]{1,0:T(8,128)(2,1)S(1)}, u32[]{:S(2)}, u32[]{:S(2)}) %collective-permute-start.10) | collective-permute-done | bytes 524320 | tf_op jit(solution)/shard_map/ppermute | solution.py:254
  85.2 3.5 fusion
  92.3 5.5 %collective-permute-done.12 = f32[144,128]{0,1:T(8,128)S(1)} collective-permute-done((f32[144,128]{0,1:T(8,128)S(1)}, f32[144,128]{0,1:T(8,128)S(1)}, u32[]{:S(2)}, u32[]{:S(2)}) %collective-permute-start.12) | collective-permute-done | bytes 73760 | tf_op jit(solution)/shard_map/ppermute | solution.py:311
  100.3 5.0 %collective-permute-done.13 = f32[144,128]{0,1:T(8,128)S(1)} collective-permute-done((f32[144,128]{0,1:T(8,128)S(1)}, f32[144,128]{0,1:T(8,128)S(1)}, u32[]{:S(2)}, u32[]{:S(2)}) %collective-permute-start.13) | collective-permute-done | bytes 73760 | tf_op jit(solution)/shard_map/ppermute | solution.py:311
  105.4 6.1 %collective-permute-start.14 = (f32[144,128]{0,1:T(8,128)S(1)}, f32[144,128]{0,1:T(8,128)S(1)}, u32[]{:S(2)}, u32[]{:S(2)}) collective-permute-start(f32[144,128]{0,1:T(8,128)S(1)} %pad_maximum_fusion.5), channel_id=1, source_target_pairs={{0,8},{8,0},{16,24},{24,16},{32,40},{40,32},{48,56},{56,48},{64,72... | collective-permute-start | bytes 221192 | tf_op jit(solution)/shard_map/ppermute | solution.py:311
  115.4 3.2 collective-permute-start.23
  118.7 9.6 %collective-permute-done.18 = f16[2048,128]{1,0:T(8,128)(2,1)} collective-permute-done((f16[2048,128]{1,0:T(8,128)(2,1)S(1)}, f16[2048,128]{1,0:T(8,128)(2,1)}, u32[]{:S(2)}, u32[]{:S(2)}) %collective-permute-start.18) | collective-permute-done | bytes 524320 | tf_op jit(solution)/shard_map/ppermute | solution.py:254
  128.4 7.7 %collective-permute-start.15 = (f32[144,128]{0,1:T(8,128)S(1)}, f32[144,128]{0,1:T(8,128)S(1)}, u32[]{:S(2)}, u32[]{:S(2)}) collective-permute-start(f32[144,128]{0,1:T(8,128)S(1)} %pad_maximum_fusion.6), channel_id=1, source_target_pairs={{0,16},{8,24},{16,0},{24,8},{32,48},{40,56},{48,32},{56,40},{64,80... | collective-permute-start | bytes 221192 | tf_op jit(solution)/shard_map/ppermute | solution.py:311
  139.0 8.0 %collective-permute-start.16 = (f32[144,128]{0,1:T(8,128)S(1)}, f32[144,128]{0,1:T(8,128)S(1)}, u32[]{:S(2)}, u32[]{:S(2)}) collective-permute-start(f32[144,128]{0,1:T(8,128)S(1)} %pad_maximum_fusion.7), channel_id=1, source_target_pairs={{0,32},{8,40},{16,48},{24,56},{32,0},{40,8},{48,16},{56,24},{64,96... | collective-permute-start | bytes 221192 | tf_op jit(solution)/shard_map/ppermute | solution.py:311
  158.8 11.7 %cholesky.17 = f32[128,128]{1,0:T(8,128)S(1)} custom-call(f32[128,128]{1,0:T(8,128)S(1)} %fusion.93), custom_call_target="Cholesky" | custom-call | tf_op jit(solution)/shard_map/jit(cholesky)/cholesky | solution.py:335
  171.9 9.8 %custom-call.6 = f32[1,128,128]{1,2,0:T(8,128)S(1)} custom-call(f32[1,128,128]{2,1,0:T(8,128)S(1)} %fusion.90), custom_call_target="InvertDiagBlocksLowerTriangular" | custom-call | tf_op jit(solution)/shard_map/triangular_solve | solution.py:336
  199.9 5.1 %collective-permute-done.22 = f16[2048,128]{1,0:T(8,128)(2,1)S(1)} collective-permute-done((f16[2048,128]{1,0:T(8,128)(2,1)}, f16[2048,128]{1,0:T(8,128)(2,1)S(1)}, u32[]{:S(2)}, u32[]{:S(2)}) %collective-permute-start.22) | collective-permute-done | bytes 524320 | tf_op jit(solution)/shard_map/ppermute | solution.py:254
  210.3 17.9 %partial_cols.3 = f32[64,256,128]{2,1,0:T(8,128)} custom-call(s32[96]{0:T(128)} %bitcast.273, s32[96]{0:T(128)} %bitcast.277, s32[5]{0:T(128)} %stack.34.refs_2_, bf16[96,256,256]{2,1,0:T(8,128)(2,1)} %bitcast.211, f32[8,256,128]{2,1,0:T(8,128)} %bitcast.217, f32[8,256,128]{2,1,0:T(8,128)} %bitcast.247, f32[8,256,128]{2,1,0:T(8,128)} %bitcast.219, ...), custom_call_target="tpu_custom_call" | custom-call | flops 1610612736 | bytes 23068672 | tf_op jit(solution)/shard_map/partial_cols/pallas_call | solution.py:195
  228.2 4.1 %fusion.2 = (f16[1,1,2,1024,128]{4,3,2,1,0:T(8,128)(2,1)S(1)}, f16[1,1,2,1024,128]{4,3,2,1,0:T(8,128)(2,1)S(1)}, f32[1,1,2,1024,128]{4,3,2,1,0:T(8,128)S(1)}, f3...) fusion(f32[4,2,2,1024,128]{4,3,2,1,0:T(8,128)} %bitcast.216, ...), kind=kLoop, calls=%fused_computation.8 | loop fusion | flops 2097152 | bytes 14680068 | tf_op jit(solution)/shard_map/convert_element_type | solution.py:223
  232.3 3.4 collective-permute-start.45
  235.8 7.1 %collective-permute-start.48 = (f16[2048,128]{1,0:T(8,128)(2,1)S(1)}, f16[2048,128]{1,0:T(8,128)(2,1)}, u32[]{:S(2)}, u32[]{:S(2)}) collective-permute-start(f16[2048,128]{1,0:T(8,128)(2,1)S(1)} %bitcast.267), channel_id=1, source_target_pairs={{0,24},{8,0},{16,8},{24,16},{32,56},{40,32},{48,40},{56,48},{64,88... | collective-permute-start | bytes 1572872 | tf_op jit(solution)/shard_map/ppermute | solution.py:260
  242.9 8.5 %partial_cols.2 = f32[64,256,128]{2,1,0:T(8,128)} custom-call(s32[96]{0:T(128)} %bitcast.274, s32[96]{0:T(128)} %bitcast.278, s32[5]{0:T(128)} %stack.34.refs_2_, bf16[96,256,256]{2,1,0:T(8,128)(2,1)} %bitcast.212, f32[8,256,128]{2,1,0:T(8,128)} %bitcast.218, f32[8,256,128]{2,1,0:T(8,128)} %bitcast.248, f32[8,256,128]{2,1,0:T(8,128)} %bitcast.220, ...), custom_call_target="tpu_custom_call" | custom-call | flops 1610612736 | bytes 23068672 | tf_op jit(solution)/shard_map/partial_cols/pallas_call | solution.py:195
  251.4 4.1 %fusion.6 = (f16[1,1,2,1024,128]{4,3,2,1,0:T(8,128)(2,1)S(1)}, f16[1,1,2,1024,128]{4,3,2,1,0:T(8,128)(2,1)S(1)}, f32[1,1,2,1024,128]{4,3,2,1,0:T(8,128)S(1)}, f3...) fusion(f32[4,2,2,1024,128]{4,3,2,1,0:T(8,128)} %bitcast.215, ...), kind=kLoop, calls=%fused_computation.16 | loop fusion | flops 2097152 | bytes 14680068 | tf_op jit(solution)/shard_map/convert_element_type | solution.py:223
  255.5 9.7 %collective-permute-start.33 = (f16[2048,128]{1,0:T(8,128)(2,1)S(1)}, f16[2048,128]{1,0:T(8,128)(2,1)S(1)}, u32[]{:S(2)}, u32[]{:S(2)}) collective-permute-start(f16[2048,128]{1,0:T(8,128)(2,1)S(1)} %bitcast.270), channel_id=1, source_target_pairs={{0,32},{8,40},{16,48},{24,56},{32,64},{40,72},{48,80},{56,88},{64,... | collective-permute-start | bytes 1572872 | tf_op jit(solution)/shard_map/ppermute | solution.py:257
  265.2 9.7 %collective-permute-start.32 = (f16[2048,128]{1,0:T(8,128)(2,1)S(1)}, f16[2048,128]{1,0:T(8,128)(2,1)S(1)}, u32[]{:S(2)}, u32[]{:S(2)}) collective-permute-start(f16[2048,128]{1,0:T(8,128)(2,1)S(1)} %bitcast.263), channel_id=1, source_target_pairs={{0,96},{8,104},{16,112},{24,120},{32,0},{40,8},{48,16},{56,24},{64... | collective-permute-start | bytes 1572872 | tf_op jit(solution)/shard_map/ppermute | solution.py:257
  279.7 6.1 %collective-permute-done.33 = f16[2048,128]{1,0:T(8,128)(2,1)S(1)} collective-permute-done((f16[2048,128]{1,0:T(8,128)(2,1)S(1)}, f16[2048,128]{1,0:T(8,128)(2,1)S(1)}, u32[]{:S(2)}, u32[]{:S(2)}) %collective-permute-start.33) | collective-permute-done | bytes 524320 | tf_op jit(solution)/shard_map/ppermute | solution.py:257
  286.0 11.4 %collective-permute-done.36 = f16[2048,128]{1,0:T(8,128)(2,1)S(1)} collective-permute-done((f16[2048,128]{1,0:T(8,128)(2,1)S(1)}, f16[2048,128]{1,0:T(8,128)(2,1)S(1)}, u32[]{:S(2)}, u32[]{:S(2)}) %collective-permute-start.36) | collective-permute-done | bytes 524320 | tf_op jit(solution)/shard_map/ppermute | solution.py:257
  304.5 9.1 %collective-permute-done.46 = f16[2048,128]{1,0:T(8,128)(2,1)S(1)} collective-permute-done((f16[2048,128]{1,0:T(8,128)(2,1)S(1)}, f16[2048,128]{1,0:T(8,128)(2,1)S(1)}, u32[]{:S(2)}, u32[]{:S(2)}) %collective-permute-start.46) | collective-permute-done | bytes 524320 | tf_op jit(solution)/shard_map/ppermute | solution.py:260
  319.5 5.1 %collective-permute-done.34 = f16[2048,128]{1,0:T(8,128)(2,1)S(1)} collective-permute-done((f16[2048,128]{1,0:T(8,128)(2,1)S(1)}, f16[2048,128]{1,0:T(8,128)(2,1)S(1)}, u32[]{:S(2)}, u32[]{:S(2)}) %collective-permute-start.34) | collective-permute-done | bytes 524320 | tf_op jit(solution)/shard_map/ppermute | solution.py:257
  331.9 3.5 collective-permute-done.42
  (173 shorter events, 112.3 us)
Async XLA Ops:
  10.1 24.9 %collective-permute-start = (f32[64,256,128]{2,1,0:T(8,128)}, f32[64,256,128]{2,1,0:T(8,128)}, u32[]{:S(2)}, u32[]{:S(2)}) collective-permute-start(f32[64,256,128]{2,1,0:T(8,128)} %get-tuple-element.7), channel_id=1, source_target_pairs={{0,1},{1,0},{2,3},{3,2},{4,5},{5,4},{6,7},{7,6},{8,9},{9,8},{10,11... | collective-permute-start | bytes 25165832 | tf_op jit(solution)/shard_map/ppermute | solution.py:251
  39.1 13.5 %collective-permute-start.6 = (f16[2048,128]{1,0:T(8,128)(2,1)S(1)}, f16[2048,128]{1,0:T(8,128)(2,1)S(1)}, u32[]{:S(2)}, u32[]{:S(2)}) collective-permute-start(f16[2048,128]{1,0:T(8,128)(2,1)S(1)} %get-tuple-element.22), channel_id=1, source_target_pairs={{0,2},{1,3},{2,4},{3,5},{4,6},{5,7},{6,0},{7,1},{8,10},{9,11},{10,... | collective-permute-start | bytes 1572872 | tf_op jit(solution)/shard_map/ppermute | solution.py:254
  40.0 16.1 %collective-permute-start.5 = (f16[2048,128]{1,0:T(8,128)(2,1)S(1)}, f16[2048,128]{1,0:T(8,128)(2,1)S(1)}, u32[]{:S(2)}, u32[]{:S(2)}) collective-permute-start(f16[2048,128]{1,0:T(8,128)(2,1)S(1)} %get-tuple-element.19), channel_id=1, source_target_pairs={{0,6},{1,7},{2,0},{3,1},{4,2},{5,3},{6,4},{7,5},{8,14},{9,15},{10,... | collective-permute-start | bytes 1572872 | tf_op jit(solution)/shard_map/ppermute | solution.py:254
  41.2 24.0 %collective-permute-start.9 = (f16[2048,128]{1,0:T(8,128)(2,1)S(1)}, f16[2048,128]{1,0:T(8,128)(2,1)S(1)}, u32[]{:S(2)}, u32[]{:S(2)}) collective-permute-start(f16[2048,128]{1,0:T(8,128)(2,1)S(1)} %get-tuple-element.20), channel_id=1, source_target_pairs={{0,6},{1,7},{2,0},{3,1},{4,2},{5,3},{6,4},{7,5},{8,14},{9,15},{10,... | collective-permute-start | bytes 1572872 | tf_op jit(solution)/shard_map/ppermute | solution.py:254
  54.1 14.9 %collective-permute-start.7 = (f16[2048,128]{1,0:T(8,128)(2,1)S(1)}, f16[2048,128]{1,0:T(8,128)(2,1)S(1)}, u32[]{:S(2)}, u32[]{:S(2)}) collective-permute-start(f16[2048,128]{1,0:T(8,128)(2,1)S(1)} %fusion.25), channel_id=1, source_target_pairs={{0,2},{1,3},{2,4},{3,5},{4,6},{5,7},{6,0},{7,1},{8,10},{9,11},{10,... | collective-permute-start | bytes 1572872 | tf_op jit(solution)/shard_map/ppermute | solution.py:254
  55.8 22.0 %collective-permute-start.8 = (f16[2048,128]{1,0:T(8,128)(2,1)S(1)}, f16[2048,128]{1,0:T(8,128)(2,1)S(1)}, u32[]{:S(2)}, u32[]{:S(2)}) collective-permute-start(f16[2048,128]{1,0:T(8,128)(2,1)S(1)} %get-tuple-element.21), channel_id=1, source_target_pairs={{0,2},{1,3},{2,4},{3,5},{4,6},{5,7},{6,0},{7,1},{8,10},{9,11},{10,... | collective-permute-start | bytes 1572872 | tf_op jit(solution)/shard_map/ppermute | solution.py:254
  112.2 16.2 %collective-permute-start.18 = (f16[2048,128]{1,0:T(8,128)(2,1)S(1)}, f16[2048,128]{1,0:T(8,128)(2,1)}, u32[]{:S(2)}, u32[]{:S(2)}) collective-permute-start(f16[2048,128]{1,0:T(8,128)(2,1)S(1)} %get-tuple-element.16), channel_id=1, source_target_pairs={{0,6},{1,7},{2,0},{3,1},{4,2},{5,3},{6,4},{7,5},{8,14},{9,15},{10,... | collective-permute-start | bytes 1572872 | tf_op jit(solution)/shard_map/ppermute | solution.py:254
  112.6 26.5 %collective-permute-start.20 = (f16[2048,128]{1,0:T(8,128)(2,1)S(1)}, f16[2048,128]{1,0:T(8,128)(2,1)}, u32[]{:S(2)}, u32[]{:S(2)}) collective-permute-start(f16[2048,128]{1,0:T(8,128)(2,1)S(1)} %get-tuple-element.16), channel_id=1, source_target_pairs={{0,2},{1,3},{2,4},{3,5},{4,6},{5,7},{6,0},{7,1},{8,10},{9,11},{10,... | collective-permute-start | bytes 1572872 | tf_op jit(solution)/shard_map/ppermute | solution.py:254
  115.4 36.6 %collective-permute-start.24 = (f16[2048,128]{1,0:T(8,128)(2,1)S(1)}, f16[2048,128]{1,0:T(8,128)(2,1)S(1)}, u32[]{:S(2)}, u32[]{:S(2)}) collective-permute-start(f16[2048,128]{1,0:T(8,128)(2,1)S(1)} %get-tuple-element.16), channel_id=1, source_target_pairs={{0,1},{1,0},{2,3},{3,2},{4,5},{5,4},{6,7},{7,6},{8,9},{9,8},{10,11... | collective-permute-start | bytes 1572872 | tf_op jit(solution)/shard_map/ppermute | solution.py:251
  115.4 71.6 %collective-permute-start.19 = (f16[2048,128]{1,0:T(8,128)(2,1)S(1)}, f16[2048,128]{1,0:T(8,128)(2,1)}, u32[]{:S(2)}, u32[]{:S(2)}) collective-permute-start(f16[2048,128]{1,0:T(8,128)(2,1)S(1)} %get-tuple-element.13), channel_id=1, source_target_pairs={{0,6},{1,7},{2,0},{3,1},{4,2},{5,3},{6,4},{7,5},{8,14},{9,15},{10,... | collective-permute-start | bytes 1572872 | tf_op jit(solution)/shard_map/ppermute | solution.py:254
  115.4 77.6 %collective-permute-start.23 = (f16[2048,128]{1,0:T(8,128)(2,1)S(1)}, f16[2048,128]{1,0:T(8,128)(2,1)}, u32[]{:S(2)}, u32[]{:S(2)}) collective-permute-start(f16[2048,128]{1,0:T(8,128)(2,1)S(1)} %get-tuple-element.13), channel_id=1, source_target_pairs={{0,2},{1,3},{2,4},{3,5},{4,6},{5,7},{6,0},{7,1},{8,10},{9,11},{10,... | collective-permute-start | bytes 1572872 | tf_op jit(solution)/shard_map/ppermute | solution.py:254
  139.0 56.1 %collective-permute-start.25 = (f16[2048,128]{1,0:T(8,128)(2,1)S(1)}, f16[2048,128]{1,0:T(8,128)(2,1)}, u32[]{:S(2)}, u32[]{:S(2)}) collective-permute-start(f16[2048,128]{1,0:T(8,128)(2,1)S(1)} %get-tuple-element.13), channel_id=1, source_target_pairs={{0,1},{1,0},{2,3},{3,2},{4,5},{5,4},{6,7},{7,6},{8,9},{9,8},{10,11... | collective-permute-start | bytes 1572872 | tf_op jit(solution)/shard_map/ppermute | solution.py:251
  151.2 38.5 %collective-permute-start.21 = (f16[2048,128]{1,0:T(8,128)(2,1)}, f16[2048,128]{1,0:T(8,128)(2,1)}, u32[]{:S(2)}, u32[]{:S(2)}) collective-permute-start(f16[2048,128]{1,0:T(8,128)(2,1)} %collective-permute-done.20), channel_id=1, source_target_pairs={{0,2},{1,3},{2,4},{3,5},{4,6},{5,7},{6,0},{7,1},{8,10},{9,11},{10,... | collective-permute-start | bytes 1572872 | tf_op jit(solution)/shard_map/ppermute | solution.py:254
  158.7 39.0 %collective-permute-start.26 = (f16[2048,128]{1,0:T(8,128)(2,1)}, f16[2048,128]{1,0:T(8,128)(2,1)S(1)}, u32[]{:S(2)}, u32[]{:S(2)}) collective-permute-start(f16[2048,128]{1,0:T(8,128)(2,1)} %collective-permute-done.18), channel_id=1, source_target_pairs={{0,1},{1,0},{2,3},{3,2},{4,5},{5,4},{6,7},{7,6},{8,9},{9,8},{10,11... | collective-permute-start | bytes 1572872 | tf_op jit(solution)/shard_map/ppermute | solution.py:251
  189.7 15.3 %collective-permute-start.22 = (f16[2048,128]{1,0:T(8,128)(2,1)}, f16[2048,128]{1,0:T(8,128)(2,1)S(1)}, u32[]{:S(2)}, u32[]{:S(2)}) collective-permute-start(f16[2048,128]{1,0:T(8,128)(2,1)} %collective-permute-done.19), channel_id=1, source_target_pairs={{0,6},{1,7},{2,0},{3,1},{4,2},{5,3},{6,4},{7,5},{8,14},{9,15},{10,... | collective-permute-start | bytes 1572872 | tf_op jit(solution)/shard_map/ppermute | solution.py:254
  193.0 13.0 %collective-permute-start.27 = (f16[2048,128]{1,0:T(8,128)(2,1)}, f16[2048,128]{1,0:T(8,128)(2,1)S(1)}, u32[]{:S(2)}, u32[]{:S(2)}) collective-permute-start(f16[2048,128]{1,0:T(8,128)(2,1)} %collective-permute-done.19), channel_id=1, source_target_pairs={{0,1},{1,0},{2,3},{3,2},{4,5},{5,4},{6,7},{7,6},{8,9},{9,8},{10,11... | collective-permute-start | bytes 1572872 | tf_op jit(solution)/shard_map/ppermute | solution.py:251
  232.3 32.9 %collective-permute-start.45 = (f16[2048,128]{1,0:T(8,128)(2,1)S(1)}, f16[2048,128]{1,0:T(8,128)(2,1)}, u32[]{:S(2)}, u32[]{:S(2)}) collective-permute-start(f16[2048,128]{1,0:T(8,128)(2,1)S(1)} %bitcast.268), channel_id=1, source_target_pairs={{0,8},{8,16},{16,24},{24,0},{32,40},{40,48},{48,56},{56,32},{64,72... | collective-permute-start | bytes 1572872 | tf_op jit(solution)/shard_map/ppermute | solution.py:260
  235.7 66.0 %collective-permute-start.44 = (f16[2048,128]{1,0:T(8,128)(2,1)S(1)}, f16[2048,128]{1,0:T(8,128)(2,1)S(1)}, u32[]{:S(2)}, u32[]{:S(2)}) collective-permute-start(f16[2048,128]{1,0:T(8,128)(2,1)S(1)} %bitcast.264), channel_id=1, source_target_pairs={{0,24},{8,0},{16,8},{24,16},{32,56},{40,32},{48,40},{56,48},{64,88... | collective-permute-start | bytes 1572872 | tf_op jit(solution)/shard_map/ppermute | solution.py:260
  235.8 40.5 %collective-permute-start.48 = (f16[2048,128]{1,0:T(8,128)(2,1)S(1)}, f16[2048,128]{1,0:T(8,128)(2,1)}, u32[]{:S(2)}, u32[]{:S(2)}) collective-permute-start(f16[2048,128]{1,0:T(8,128)(2,1)S(1)} %bitcast.267), channel_id=1, source_target_pairs={{0,24},{8,0},{16,8},{24,16},{32,56},{40,32},{48,40},{56,48},{64,88... | collective-permute-start | bytes 1572872 | tf_op jit(solution)/shard_map/ppermute | solution.py:260
  242.9 56.7 %collective-permute-start.47 = (f16[2048,128]{1,0:T(8,128)(2,1)S(1)}, f16[2048,128]{1,0:T(8,128)(2,1)}, u32[]{:S(2)}, u32[]{:S(2)}) collective-permute-start(f16[2048,128]{1,0:T(8,128)(2,1)S(1)} %bitcast.266), channel_id=1, source_target_pairs={{0,8},{8,16},{16,24},{24,0},{32,40},{40,48},{48,56},{56,32},{64,72... | collective-permute-start | bytes 1572872 | tf_op jit(solution)/shard_map/ppermute | solution.py:260
  255.5 30.3 %collective-permute-start.33 = (f16[2048,128]{1,0:T(8,128)(2,1)S(1)}, f16[2048,128]{1,0:T(8,128)(2,1)S(1)}, u32[]{:S(2)}, u32[]{:S(2)}) collective-permute-start(f16[2048,128]{1,0:T(8,128)(2,1)S(1)} %bitcast.270), channel_id=1, source_target_pairs={{0,32},{8,40},{16,48},{24,56},{32,64},{40,72},{48,80},{56,88},{64,... | collective-permute-start | bytes 1572872 | tf_op jit(solution)/shard_map/ppermute | solution.py:257
  265.2 53.3 %collective-permute-start.32 = (f16[2048,128]{1,0:T(8,128)(2,1)S(1)}, f16[2048,128]{1,0:T(8,128)(2,1)S(1)}, u32[]{:S(2)}, u32[]{:S(2)}) collective-permute-start(f16[2048,128]{1,0:T(8,128)(2,1)S(1)} %bitcast.263), channel_id=1, source_target_pairs={{0,96},{8,104},{16,112},{24,120},{32,0},{40,8},{48,16},{56,24},{64... | collective-permute-start | bytes 1572872 | tf_op jit(solution)/shard_map/ppermute | solution.py:257
  276.3 21.1 %collective-permute-start.36 = (f16[2048,128]{1,0:T(8,128)(2,1)S(1)}, f16[2048,128]{1,0:T(8,128)(2,1)S(1)}, u32[]{:S(2)}, u32[]{:S(2)}) collective-permute-start(f16[2048,128]{1,0:T(8,128)(2,1)S(1)} %bitcast.269), channel_id=1, source_target_pairs={{0,96},{8,104},{16,112},{24,120},{32,0},{40,8},{48,16},{56,24},{64... | collective-permute-start | bytes 1572872 | tf_op jit(solution)/shard_map/ppermute | solution.py:257
  285.8 13.9 %collective-permute-start.49 = (f16[2048,128]{1,0:T(8,128)(2,1)S(1)}, f16[2048,128]{1,0:T(8,128)(2,1)S(1)}, u32[]{:S(2)}, u32[]{:S(2)}) collective-permute-start(f16[2048,128]{1,0:T(8,128)(2,1)S(1)} %fusion.39), channel_id=1, source_target_pairs={{0,24},{8,0},{16,8},{24,16},{32,56},{40,32},{48,40},{56,48},{64,88... | collective-permute-start | bytes 1572872 | tf_op jit(solution)/shard_map/ppermute | solution.py:260
  297.4 16.7 %collective-permute-start.35 = (f16[2048,128]{1,0:T(8,128)(2,1)S(1)}, f16[2048,128]{1,0:T(8,128)(2,1)S(1)}, u32[]{:S(2)}, u32[]{:S(2)}) collective-permute-start(f16[2048,128]{1,0:T(8,128)(2,1)S(1)} %bitcast.265), channel_id=1, source_target_pairs={{0,32},{8,40},{16,48},{24,56},{32,64},{40,72},{48,80},{56,88},{64,... | collective-permute-start | bytes 1572872 | tf_op jit(solution)/shard_map/ppermute | solution.py:257
  299.6 14.0 %collective-permute-start.46 = (f16[2048,128]{1,0:T(8,128)(2,1)S(1)}, f16[2048,128]{1,0:T(8,128)(2,1)S(1)}, u32[]{:S(2)}, u32[]{:S(2)}) collective-permute-start(f16[2048,128]{1,0:T(8,128)(2,1)S(1)} %fusion.42), channel_id=1, source_target_pairs={{0,8},{8,16},{16,24},{24,0},{32,40},{40,48},{48,56},{56,32},{64,72... | collective-permute-start | bytes 1572872 | tf_op jit(solution)/shard_map/ppermute | solution.py:260
  299.7 25.0 %collective-permute-start.34 = (f16[2048,128]{1,0:T(8,128)(2,1)S(1)}, f16[2048,128]{1,0:T(8,128)(2,1)S(1)}, u32[]{:S(2)}, u32[]{:S(2)}) collective-permute-start(f16[2048,128]{1,0:T(8,128)(2,1)S(1)} %fusion.48), channel_id=1, source_target_pairs={{0,32},{8,40},{16,48},{24,56},{32,64},{40,72},{48,80},{56,88},{64,... | collective-permute-start | bytes 1572872 | tf_op jit(solution)/shard_map/ppermute | solution.py:257
  301.7 15.4 %collective-permute-start.37 = (f16[2048,128]{1,0:T(8,128)(2,1)S(1)}, f16[2048,128]{1,0:T(8,128)(2,1)S(1)}, u32[]{:S(2)}, u32[]{:S(2)}) collective-permute-start(f16[2048,128]{1,0:T(8,128)(2,1)S(1)} %fusion.45), channel_id=1, source_target_pairs={{0,96},{8,104},{16,112},{24,120},{32,0},{40,8},{48,16},{56,24},{64... | collective-permute-start | bytes 1572872 | tf_op jit(solution)/shard_map/ppermute | solution.py:257
  313.6 13.9 %collective-permute-start.51 = (f16[512,128]{1,0:T(8,128)(2,1)S(1)}, f16[512,128]{1,0:T(8,128)(2,1)S(1)}, u32[]{:S(2)}, u32[]{:S(2)}) collective-permute-start(f16[512,128]{1,0:T(8,128)(2,1)S(1)} %get-tuple-element.48), channel_id=1, source_target_pairs={{0,32},{8,40},{16,48},{24,56},{32,64},{40,72},{48,80},{56,88},{64,... | collective-permute-start | bytes 393224 | tf_op jit(solution)/shard_map/ppermute | solution.py:257
  314.1 21.3 %collective-permute-start.50 = (f16[512,128]{1,0:T(8,128)(2,1)S(1)}, f16[512,128]{1,0:T(8,128)(2,1)S(1)}, u32[]{:S(2)}, u32[]{:S(2)}) collective-permute-start(f16[512,128]{1,0:T(8,128)(2,1)S(1)} %get-tuple-element.46), channel_id=1, source_target_pairs={{0,96},{8,104},{16,112},{24,120},{32,0},{40,8},{48,16},{56,24},{64... | collective-permute-start | bytes 393224 | tf_op jit(solution)/shard_map/ppermute | solution.py:257
  318.6 16.9 %collective-permute-start.53 = (f16[512,128]{1,0:T(8,128)(2,1)S(1)}, f16[512,128]{1,0:T(8,128)(2,1)S(1)}, u32[]{:S(2)}, u32[]{:S(2)}) collective-permute-start(f16[512,128]{1,0:T(8,128)(2,1)S(1)} %fusion.88), channel_id=1, source_target_pairs={{0,32},{8,40},{16,48},{24,56},{32,64},{40,72},{48,80},{56,88},{64,... | collective-permute-start | bytes 393224 | tf_op jit(solution)/shard_map/ppermute | solution.py:257
  327.4 13.3 %collective-permute-start.38 = (f16[512,128]{1,0:T(8,128)(2,1)S(1)}, f16[512,128]{1,0:T(8,128)(2,1)S(1)}, u32[]{:S(2)}, u32[]{:S(2)}) collective-permute-start(f16[512,128]{1,0:T(8,128)(2,1)S(1)} %get-tuple-element.41), channel_id=1, source_target_pairs={{0,24},{8,0},{16,8},{24,16},{32,56},{40,32},{48,40},{56,48},{64,88... | collective-permute-start | bytes 393224 | tf_op jit(solution)/shard_map/ppermute | solution.py:260
  (26 other events, 209.9 us)
